TPU v7x, 32 devices: a whole 2x2x4 slice. The times are simulated.
32 devices in a mesh: shift: 4 (over y, x), rows: 8 (over z, core).
Axes of the slice: x: 2, y: 2, z: 4, core: 2. Of those that a mesh axis runs over, the one named last changes fastest.
Arguments:
- zc_in: bfloat16 [4, 512, 16384], P('shift', 'rows'), may hold values from -6 to 6
- zo_in: bfloat16 [4, 384, 16384], P('shift', 'rows'), may hold values from -6 to 6
- count_c: int32 [4], replicated, may hold values from 256 to 512, as said below
- count_o: int32 [4], replicated, may hold values from 192 to 384, as said below
- mass: bfloat16 [128, 4, 128, 128], P(('shift', 'rows')), may hold values from -0.25 to 0.25
- adjacency: int32 [128, 4], P(('shift', 'rows')), may hold values from 0 to 127, as said below
- ghost_len: int32 [128, 4], P(('shift', 'rows')), may hold values from 1 to 128, as said below
- omega: float32 [2048, 128], replicated, may hold values from -6 to 6
Outputs:
- proj_c: float32 [128, 16384], P(None, ('shift', 'rows'))
- proj_o: float32 [128, 16384], P(None, ('shift', 'rows'))
Inputs may be any that keep to these rules, and one draw needn't show every extreme that they name: `count_c`: each entry is 256 or more, and one group holds 512 exactly. `count_o`: each entry is 192 or more, and one group holds 384 exactly. adjacency[i, 0] = i, and every entry lies within 2 blocks of i. ghost_len[i, 0] = 128.
All inputs are finite; a program needn't handle non-finite values.
Results may differ from a plain program's by a relative error of at most 0.0047.
Values may be sent and summed in bfloat16 or wider, within the bound.
A program may use at most 128 MiB of HBM per device.

v0:
```python
import jax
import jax.numpy as jnp
from jax import lax
from jax.sharding import PartitionSpec as P

REACH = 2


def padded(shard, sides, width):
    for axis, dim in sides:
        size, length = (lax.axis_size(axis), shard.shape[dim])
        up = [(i, (i + 1) % size) for i in range(size - 1)]
        down = [(j, i) for i, j in up]
        last = lax.slice_in_dim(shard, length - width, length, axis=dim)
        initial = lax.slice_in_dim(shard, 0, width, axis=dim)
        before = lax.ppermute(last, axis, up)
        after = lax.ppermute(initial, axis, down)
        shard = jnp.concatenate([before, shard, after], axis=dim)
    return shard


def prepare(factor, counts, group, member):
    width = factor.shape[1]
    slots = member * width + jnp.arange(width, dtype=jnp.int32)
    keep = slots < counts[group]
    return jnp.where(keep[:, None], factor[0], jnp.zeros_like(factor[0]))


def orth_local(matrix):
    square = jnp.dot(matrix.T, matrix, precision=lax.Precision.HIGHEST)
    lower = jnp.linalg.cholesky(square)
    return jax.scipy.linalg.solve_triangular(lower, matrix.T, lower=True).T


def per_device(zc_in, zo_in, count_c, count_o, mass, adjacency, ghost_len, omega):
    group = lax.axis_index("shift")
    member = lax.axis_index("rows")
    members = lax.axis_size("rows")
    part_c = prepare(zc_in, count_c, group, member)
    part_o = prepare(zo_in, count_o, group, member)
    zc, zo = (
        lax.all_to_all(part_c, ("shift", "rows"), split_axis=1, concat_axis=0, tiled=True),
        lax.all_to_all(part_o, ("shift", "rows"), split_axis=1, concat_axis=0, tiled=True),
    )
    width_c = zc.shape[0]
    rows_here = zc.shape[1]
    block_size = mass.shape[2]
    count_blocks = rows_here // block_size
    extended = padded(zc, ((("shift", "rows"), 1),), REACH * block_size)
    first_block = (group * members + member) * count_blocks
    local_index = (adjacency - first_block + REACH).reshape(-1)
    blocks = extended.reshape(width_c, count_blocks + 2 * REACH, block_size)
    pieces = jnp.take(blocks, local_index, axis=1).reshape(
        width_c, count_blocks, adjacency.shape[1], block_size
    )
    inner = jnp.arange(block_size, dtype=jnp.int32)
    keep = inner[None, None, None, :] < ghost_len[:, :, None, None]
    masked = jnp.where(keep, mass, jnp.zeros_like(mass))
    mixed = jnp.einsum("cikp,ikqp->ciq", pieces, masked, preferred_element_type=jnp.float32)
    mixed = mixed.astype(jnp.bfloat16).reshape(width_c, rows_here)
    high = lax.Precision.HIGHEST
    partial_gram = lax.dot_general(
        zo, mixed, (((1,), (1,)), ((), ())), preferred_element_type=jnp.float32
    )
    gram = lax.psum(partial_gram, ("shift", "rows"))
    first = orth_local(jnp.dot(gram, omega, precision=high))
    right = orth_local(jnp.dot(gram.T, first, precision=high))
    left = orth_local(jnp.dot(gram, right, precision=high))
    proj_c = jnp.dot(right.astype(jnp.bfloat16).T, zc, preferred_element_type=jnp.float32)
    proj_o = jnp.dot(left.astype(jnp.bfloat16).T, zo, preferred_element_type=jnp.float32)
    return (proj_c, proj_o)


def solution(mesh):
    placed = (
        P("shift", "rows", None),
        P("shift", "rows", None),
        P(),
        P(),
        P(("shift", "rows"), None, None, None),
        P(("shift", "rows"), None),
        P(("shift", "rows"), None),
        P(),
    )
    return jax.shard_map(
        per_device,
        mesh=mesh,
        in_specs=placed,
        out_specs=(P(None, ("shift", "rows")), P(None, ("shift", "rows"))),
        check_vma=False,
    )
```

profile of v0, /device:TPU:0, one launch (start us, length us, event | category | flops | bytes accessed | tf_op | source)
XLA Modules:
  0.0 544.3 jit_solution(15689129905431404123)
XLA Ops:
  7.2 2.4 copy.32
  11.3 2.5 copy.24
  13.8 7.3 %all-to-all-start.1 = ((bf16[64,32,512]{2,0,1:T(8,128)(2,1)}), bf16[64,32,512]{2,0,1:T(8,128)(2,1)S(1)}, u32[]{:S(2)}, u32[]{:S(2)}) async-start(bf16[64,32,512]{2,0,1:T(8,128)(2,1)} %copy.24), calls=%async_computation.1 | async-start | bytes 4194304 | tf_op jit(solution)/shard_map/all_to_all | solution.py:42
  26.7 44.5 %all-to-all-done.1 = bf16[64,32,512]{2,0,1:T(8,128)(2,1)S(1)} async-done(((bf16[64,32,512]{2,0,1:T(8,128)(2,1)}), bf16[64,32,512]{2,0,1:T(8,128)(2,1)S(1)}, u32[]{:S(2)}, u32[]{:S(2)}) %all-to-all-start.1) | async-done | bytes 2097184 | tf_op jit(solution)/shard_map/all_to_all | solution.py:42
  71.2 3.4 all-to-all-start
  76.2 3.0 collective-permute-start
  80.8 3.4 collective-permute-done.1
  84.2 3.4 pad_maximum_fusion
  87.6 6.5 %copy.25 = bf16[2048,1024]{0,1:T(8,128)(2,1)} copy(bf16[2048,1024]{1,0:T(8,128)(2,1)} %pad_maximum_fusion) | data formatting | bytes 8388608 | tf_op jit(solution)/shard_map/concatenate | solution.py:18
  94.1 6.5 %copy.26 = bf16[2048,8,128]{2,0,1:T(8,128)(2,1)} copy(bf16[2048,8,128]{0,2,1:T(8,128)(2,1)} %bitcast.82) | data formatting | bytes 8388608 | tf_op jit(solution)/shard_map/reshape | solution.py:52
  100.6 6.9 %gather_fusion = bf16[16,2048,128]{2,1,0:T(8,128)(2,1)} fusion(bf16[2048,8,128]{2,0,1:T(8,128)(2,1)} %copy.26, s32[1024]{0:T(1024)S(1)} %pad_clamp_fusion), kind=kCustom, calls=%fused_computation | custom fusion | bytes 16777280 | tf_op jit(solution)/shard_map/jit(_take)/gather | solution.py:53
  107.5 7.8 %bitcast_convert_fusion = bf16[4,128,2048]{2,1,0:T(8,128)(2,1)} fusion(bf16[2048,4,4,128]{3,0,2,1:T(8,128)(2,1)} %bitcast.83, pred[4,4]{1,0:T(4,128)(4,1)S(1)} %compare_and_fusion, bf16[4,4,128,128]{3,2,1,0:T(8,128)(2,1)} %param.15, pred[4,4,128]{2,1,0:T(4,128)(4,1)S(1)} %iota_compare_fusion.2), kind=kOutput, calls=%fused_computation.5 | convolution fusion | flops 1079246848 | bytes 11012112 | tf_op jit(solution)/shard_map/cikp,ikqp->ciq/dot_general | solution.py:59
  115.3 10.0 %fusion.30 = f32[1536,2048]{1,0:T(8,128)} fusion(bf16[1536,512]{1,0:T(8,128)(2,1)} %bitcast.2, bf16[2048,512]{0,1:T(8,128)(2,1)} %bitcast.86), kind=kOutput, calls=%fused_computation.55 | convolution fusion | flops 3221225472 | bytes 16252928 | tf_op jit(solution)/shard_map/dot_general | solution.py:62
  125.4 278.8 %all-reduce.2.cloned.1.call-done = f32[1536,2048]{1,0:T(8,128)} async-done(((f32[1536,2048]{1,0:T(8,128)}), f32[1536,2048]{1,0:T(8,128)}) %all-reduce.2.cloned.1.call-update) | async-done | bytes 12582928 | tf_op jit(solution)/shard_map/psum | solution.py:65
  404.1 12.7 %fusion.31 = f32[1536,128]{1,0:T(8,128)S(1)} fusion(f32[1536,2048]{1,0:T(8,128)} %all-reduce.2.cloned.1.call-done, f32[2048,128]{1,0:T(8,128)S(1)} %copy-done), kind=kOutput, calls=%fused_computation.56 | convolution fusion | flops 4831838208 | bytes 14417920 | tf_op jit(solution)/shard_map/dot_general | solution.py:66
  419.3 11.7 %cholesky.59 = f32[128,128]{1,0:T(8,128)S(1)} custom-call(f32[128,128]{1,0:T(8,128)S(1)} %fusion.23), custom_call_target="Cholesky" | custom-call | tf_op jit(solution)/shard_map/jit(cholesky)/cholesky | solution.py:31
  432.4 9.8 %custom-call.11 = f32[1,128,128]{1,2,0:T(8,128)S(1)} custom-call(f32[1,128,128]{2,1,0:T(8,128)S(1)} %fusion.14), custom_call_target="InvertDiagBlocksLowerTriangular" | custom-call | tf_op jit(solution)/shard_map/jit(_solve_triangular)/triangular_solve | solution.py:32
  444.2 23.2 %fusion.33 = f32[2048,128]{1,0:T(8,128)S(1)} fusion(f32[1536,2048]{1,0:T(8,128)} %all-reduce.2.cloned.1.call-done, f32[128,1536]{1,0:T(8,128)S(1)} %fusion.7), kind=kOutput, calls=%fused_computation.58 | convolution fusion | flops 4831838208 | bytes 14417920 | tf_op jit(solution)/shard_map/dot_general | solution.py:67
  470.5 11.7 %cholesky.70 = f32[128,128]{1,0:T(8,128)S(1)} custom-call(f32[128,128]{1,0:T(8,128)S(1)} %fusion.21), custom_call_target="Cholesky" | custom-call | tf_op jit(solution)/shard_map/jit(cholesky)/cholesky | solution.py:31
  483.5 9.8 %custom-call.9 = f32[1,128,128]{1,2,0:T(8,128)S(1)} custom-call(f32[1,128,128]{2,1,0:T(8,128)S(1)} %fusion.15), custom_call_target="InvertDiagBlocksLowerTriangular" | custom-call | tf_op jit(solution)/shard_map/jit(_solve_triangular)/triangular_solve | solution.py:32
  496.8 12.7 %fusion.35 = f32[1536,128]{1,0:T(8,128)S(1)} fusion(f32[1536,2048]{1,0:T(8,128)} %all-reduce.2.cloned.1.call-done, f32[128,2048]{1,0:T(8,128)S(1)} %fusion.19), kind=kOutput, calls=%fused_computation.60 | convolution fusion | flops 4831838208 | bytes 14417920 | tf_op jit(solution)/shard_map/dot_general | solution.py:68
  511.0 11.7 %cholesky.81 = f32[128,128]{1,0:T(8,128)S(1)} custom-call(f32[128,128]{1,0:T(8,128)S(1)} %fusion.18), custom_call_target="Cholesky" | custom-call | tf_op jit(solution)/shard_map/jit(cholesky)/cholesky | solution.py:31
  524.1 9.8 %custom-call.12 = f32[1,128,128]{1,2,0:T(8,128)S(1)} custom-call(f32[1,128,128]{2,1,0:T(8,128)S(1)} %fusion.16), custom_call_target="InvertDiagBlocksLowerTriangular" | custom-call | tf_op jit(solution)/shard_map/jit(_solve_triangular)/triangular_solve | solution.py:32
  534.8 2.5 fusion.37
  (56 shorter events, 27.7 us)
Async XLA Ops:
  7.2 397.0 %copy-start = (f32[2048,128]{1,0:T(8,128)S(1)}, f32[2048,128]{1,0:T(8,128)}, u32[]{:S(2)}) copy-start(f32[2048,128]{1,0:T(8,128)} %param.18) | copy-start | bytes 3145732
  7.2 2.5 copy-start.5
  11.3 9.8 %copy-start.6 = (s32[4]{0:T(128)S(1)}, s32[4]{0:T(128)}, u32[]{:S(2)}) copy-start(s32[4]{0:T(128)} %param.14) | copy-start | bytes 52
  13.8 57.4 %all-to-all-start.1 = ((bf16[64,32,512]{2,0,1:T(8,128)(2,1)}), bf16[64,32,512]{2,0,1:T(8,128)(2,1)S(1)}, u32[]{:S(2)}, u32[]{:S(2)}) async-start(bf16[64,32,512]{2,0,1:T(8,128)(2,1)} %copy.24), calls=%async_computation.1 | async-start | bytes 4194304 | tf_op jit(solution)/shard_map/all_to_all | solution.py:42
  26.7 53.9 %copy-start.3 = (s32[4,4]{1,0:T(4,128)S(1)}, s32[4,4]{1,0:T(4,128)}, u32[]{:S(2)}) copy-start(s32[4,4]{1,0:T(4,128)} %param.16) | copy-start | bytes 196
  26.7 54.0 %copy-start.4 = (s32[4,4]{1,0:T(4,128)S(1)}, s32[4,4]{1,0:T(4,128)}, u32[]{:S(2)}) copy-start(s32[4,4]{1,0:T(4,128)} %param.17) | copy-start | bytes 196
  71.2 44.1 %all-to-all-start = ((bf16[48,32,512]{2,0,1:T(8,128)(2,1)}), bf16[48,32,512]{2,0,1:T(8,128)(2,1)}, u32[]{:S(2)}, u32[]{:S(2)}) async-start(bf16[48,32,512]{2,0,1:T(8,128)(2,1)} %copy.23), calls=%async_computation | async-start | bytes 3145728 | tf_op jit(solution)/shard_map/all_to_all | solution.py:43
  74.6 329.5 %all-reduce.2.cloned.1.call-start = ((), (), s32[]{:S(2)}) async-start(), calls=%async_computation.2 | async-start | bytes 25165824 | tf_op jit(solution)/shard_map/psum | solution.py:65
  76.2 4.7 collective-permute-start
  79.1 5.1 collective-permute-start.1
  416.8 0.9 copy-start.2
  467.4 1.1 copy-start.1
Sparse Core Ops, SparseCore 0:
  125.5 278.5 all-reduce.1
where the time goes:
time: 549 us; the launch traced here: 544 us
  waiting for transfers between devices  327 us (60%)
  matrix products  80 us (15%)
  other arithmetic  74.1 us (13%)
  local copies, waits for them, and re-layouts  33.9 us (6%)
  starting transfers between devices  15.2 us (3%)
  between operations  14.6 us (3%)
    psum x1, waiting for transfers between devices, per_device(): gram = lax.psum(partial_gram, ('shift', 'rows'))  279 us
    all_to_all x1, waiting for transfers between devices, per_device(): lax.all_to_all(part_c, ('shift', 'rows'), split_axis=1, concat_axis=0, ti...  44.5 us
    another operation x9, other arithmetic, orth_local(): lower = jnp.linalg.cholesky(square)  37.2 us
    another operation x6, other arithmetic, orth_local(): return jax.scipy.linalg.solve_triangular(lower, matrix.T, lower=True).T  31.4 us
    dot_general x1, matrix products, per_device(): right = orth_local(jnp.dot(gram.T, first, precision=high))  23.2 us
    dot_general x1, matrix products, per_device(): first = orth_local(jnp.dot(gram, omega, precision=high))  12.7 us
    dot_general x1, matrix products, per_device(): left = orth_local(jnp.dot(gram, right, precision=high))  12.7 us
  transfers between devices with their start and end apart: 5, of which 3 were waited for; matrix products, arithmetic and copies ran while one was open for 7% of the time, Pallas kernels for 0%

commit v1 on v0

--- a/solution.py
+++ b/solution.py
@@ -62,7 +62,7 @@
     partial_gram = lax.dot_general(
         zo, mixed, (((1,), (1,)), ((), ())), preferred_element_type=jnp.float32
     )
-    gram = lax.psum(partial_gram, ("shift", "rows"))
+    gram = lax.psum(lax.psum(partial_gram, "rows"), "shift")
     first = orth_local(jnp.dot(gram, omega, precision=high))
     right = orth_local(jnp.dot(gram.T, first, precision=high))
     left = orth_local(jnp.dot(gram, right, precision=high))

time: 549 us -> 821 us (1.50)
  waiting for transfers between devices: 327 us -> 595 us
    psum x1 -> x2, waiting for transfers between devices: 279 us -> 546 us  [per_device(): gram = lax.psum(lax.psum(partial_gram, 'rows'), 'shift')]
  transfers between devices with their start and end apart: 5 -> 6, of which waited for: 3 -> 5; matrix products, arithmetic and copies ran while one was open for 7% -> 5% of each run, Pallas kernels for 0% -> 0%
where the time goes in v1:
time: 821 us; the launch traced here: 812 us
  waiting for transfers between devices  595 us (72%)
  matrix products  79.9 us (10%)
  other arithmetic  74.1 us (9%)
  local copies, waits for them, and re-layouts  33.8 us (4%)
  starting transfers between devices  15 us (2%)
  between operations  14.5 us (2%)
    psum x2, waiting for transfers between devices, per_device(): gram = lax.psum(lax.psum(partial_gram, 'rows'), 'shift')  546 us
    all_to_all x1, waiting for transfers between devices, per_device(): lax.all_to_all(part_c, ('shift', 'rows'), split_axis=1, concat_axis=0, ti...  44.5 us
    another operation x9, other arithmetic, orth_local(): lower = jnp.linalg.cholesky(square)  37.2 us
    another operation x6, other arithmetic, orth_local(): return jax.scipy.linalg.solve_triangular(lower, matrix.T, lower=True).T  31.4 us
    dot_general x1, matrix products, per_device(): right = orth_local(jnp.dot(gram.T, first, precision=high))  23.3 us
  transfers between devices with their start and end apart: 6, of which 5 were waited for; matrix products, arithmetic and copies ran while one was open for 5% of the time, Pallas kernels for 0%

profile of v1, /device:TPU:0, one launch (start us, length us, event | category | flops | bytes accessed | tf_op | source)
XLA Modules:
  0.0 812.0 jit_solution(13888235836365079452)
XLA Ops:
  11.3 2.5 copy.24
  13.8 7.3 all-to-all-start.1
  26.7 44.5 %all-to-all-done.1 = bf16[64,32,512]{2,0,1:T(8,128)(2,1)S(1)} async-done(((bf16[64,32,512]{2,0,1:T(8,128)(2,1)}), bf16[64,32,512]{2,0,1:T(8,128)(2,1)S(1)}, u32[]{:S(2)}, u32[]{:S(2)}) %all-to-all-start.1) | async-done | bytes 2097184 | tf_op jit(solution)/shard_map/all_to_all | solution.py:42
  71.2 3.4 all-to-all-start
  76.1 2.9 collective-permute-start
  80.7 3.5 collective-permute-done.1
  84.2 3.4 pad_maximum_fusion
  87.6 6.5 copy.25
  94.1 6.5 copy.26
  100.6 6.9 gather_fusion
  107.5 7.8 bitcast_convert_fusion
  115.3 10.1 %fusion.30 = f32[1536,2048]{1,0:T(8,128)} fusion(bf16[1536,512]{1,0:T(8,128)(2,1)} %bitcast.2, bf16[2048,512]{0,1:T(8,128)(2,1)} %bitcast.86), kind=kOutput, calls=%fused_computation.55 | convolution fusion | flops 3221225472 | bytes 16252928 | tf_op jit(solution)/shard_map/dot_general | solution.py:62
  125.4 303.2 %all-reduce.3.cloned.1.call-done = f32[1536,2048]{1,0:T(8,128)} async-done(((f32[1536,2048]{1,0:T(8,128)}), f32[1536,2048]{1,0:T(8,128)}) %all-reduce.3.cloned.1.call-update) | async-done | bytes 12582928 | tf_op jit(solution)/shard_map/psum | solution.py:65
  428.7 243.2 %all-reduce.5.cloned.1.call-done = f32[1536,2048]{1,0:T(8,128)} async-done(((f32[1536,2048]{1,0:T(8,128)}), f32[1536,2048]{1,0:T(8,128)}) %all-reduce.5.cloned.1.call-update) | async-done | bytes 12582928 | tf_op jit(solution)/shard_map/psum | solution.py:65
  671.9 12.6 %fusion.31 = f32[1536,128]{1,0:T(8,128)S(1)} fusion(f32[1536,2048]{1,0:T(8,128)} %all-reduce.5.cloned.1.call-done, f32[2048,128]{1,0:T(8,128)S(1)} %copy-done), kind=kOutput, calls=%fused_computation.56 | convolution fusion | flops 4831838208 | bytes 14417920 | tf_op jit(solution)/shard_map/dot_general | solution.py:66
  687.0 11.7 %cholesky.59 = f32[128,128]{1,0:T(8,128)S(1)} custom-call(f32[128,128]{1,0:T(8,128)S(1)} %fusion.23), custom_call_target="Cholesky" | custom-call | tf_op jit(solution)/shard_map/jit(cholesky)/cholesky | solution.py:31
  700.1 9.8 %custom-call.11 = f32[1,128,128]{1,2,0:T(8,128)S(1)} custom-call(f32[1,128,128]{2,1,0:T(8,128)S(1)} %fusion.14), custom_call_target="InvertDiagBlocksLowerTriangular" | custom-call | tf_op jit(solution)/shard_map/jit(_solve_triangular)/triangular_solve | solution.py:32
  711.9 23.3 %fusion.33 = f32[2048,128]{1,0:T(8,128)S(1)} fusion(f32[1536,2048]{1,0:T(8,128)} %all-reduce.5.cloned.1.call-done, f32[128,1536]{1,0:T(8,128)S(1)} %fusion.7), kind=kOutput, calls=%fused_computation.58 | convolution fusion | flops 4831838208 | bytes 14417920 | tf_op jit(solution)/shard_map/dot_general | solution.py:67
  738.2 11.7 %cholesky.70 = f32[128,128]{1,0:T(8,128)S(1)} custom-call(f32[128,128]{1,0:T(8,128)S(1)} %fusion.21), custom_call_target="Cholesky" | custom-call | tf_op jit(solution)/shard_map/jit(cholesky)/cholesky | solution.py:31
  751.3 9.8 %custom-call.9 = f32[1,128,128]{1,2,0:T(8,128)S(1)} custom-call(f32[1,128,128]{2,1,0:T(8,128)S(1)} %fusion.15), custom_call_target="InvertDiagBlocksLowerTriangular" | custom-call | tf_op jit(solution)/shard_map/jit(_solve_triangular)/triangular_solve | solution.py:32
  764.6 12.6 %fusion.35 = f32[1536,128]{1,0:T(8,128)S(1)} fusion(f32[1536,2048]{1,0:T(8,128)} %all-reduce.5.cloned.1.call-done, f32[128,2048]{1,0:T(8,128)S(1)} %fusion.19), kind=kOutput, calls=%fused_computation.60 | convolution fusion | flops 4831838208 | bytes 14417920 | tf_op jit(solution)/shard_map/dot_general | solution.py:68
  778.7 11.7 %cholesky.81 = f32[128,128]{1,0:T(8,128)S(1)} custom-call(f32[128,128]{1,0:T(8,128)S(1)} %fusion.18), custom_call_target="Cholesky" | custom-call | tf_op jit(solution)/shard_map/jit(cholesky)/cholesky | solution.py:31
  791.8 9.8 %custom-call.12 = f32[1,128,128]{1,2,0:T(8,128)S(1)} custom-call(f32[1,128,128]{2,1,0:T(8,128)S(1)} %fusion.16), custom_call_target="InvertDiagBlocksLowerTriangular" | custom-call | tf_op jit(solution)/shard_map/jit(_solve_triangular)/triangular_solve | solution.py:32
  802.5 2.5 fusion.37
  (59 shorter events, 30.1 us)
Async XLA Ops:
  7.2 664.7 %copy-start = (f32[2048,128]{1,0:T(8,128)S(1)}, f32[2048,128]{1,0:T(8,128)}, u32[]{:S(2)}) copy-start(f32[2048,128]{1,0:T(8,128)} %param.18) | copy-start | bytes 3145732
  7.2 2.5 copy-start.5
  11.3 9.8 %copy-start.6 = (s32[4]{0:T(128)S(1)}, s32[4]{0:T(128)}, u32[]{:S(2)}) copy-start(s32[4]{0:T(128)} %param.14) | copy-start | bytes 52
  13.8 57.4 %all-to-all-start.1 = ((bf16[64,32,512]{2,0,1:T(8,128)(2,1)}), bf16[64,32,512]{2,0,1:T(8,128)(2,1)S(1)}, u32[]{:S(2)}, u32[]{:S(2)}) async-start(bf16[64,32,512]{2,0,1:T(8,128)(2,1)} %copy.24), calls=%async_computation.1 | async-start | bytes 4194304 | tf_op jit(solution)/shard_map/all_to_all | solution.py:42
  26.7 53.7 %copy-start.3 = (s32[4,4]{1,0:T(4,128)S(1)}, s32[4,4]{1,0:T(4,128)}, u32[]{:S(2)}) copy-start(s32[4,4]{1,0:T(4,128)} %param.16) | copy-start | bytes 196
  26.7 53.8 %copy-start.4 = (s32[4,4]{1,0:T(4,128)S(1)}, s32[4,4]{1,0:T(4,128)}, u32[]{:S(2)}) copy-start(s32[4,4]{1,0:T(4,128)} %param.17) | copy-start | bytes 196
  71.2 44.1 %all-to-all-start = ((bf16[48,32,512]{2,0,1:T(8,128)(2,1)}), bf16[48,32,512]{2,0,1:T(8,128)(2,1)}, u32[]{:S(2)}, u32[]{:S(2)}) async-start(bf16[48,32,512]{2,0,1:T(8,128)(2,1)} %copy.23), calls=%async_computation | async-start | bytes 3145728 | tf_op jit(solution)/shard_map/all_to_all | solution.py:43
  74.6 354.0 %all-reduce.3.cloned.1.call-start = ((), (), s32[]{:S(2)}) async-start(), calls=%async_computation.2 | async-start | bytes 25165824 | tf_op jit(solution)/shard_map/psum | solution.py:65
  76.1 4.6 collective-permute-start
  79.1 5.1 collective-permute-start.1
  125.4 546.5 %all-reduce.5.cloned.1.call-start = ((), (), s32[]{:S(2)}) async-start(), calls=%async_computation.3 | async-start | bytes 25165824 | tf_op jit(solution)/shard_map/psum | solution.py:65
  684.5 0.9 copy-start.2
  735.2 1.1 copy-start.1
Sparse Core Ops, SparseCore 0:
  125.5 303.1 all-reduce.2
  432.1 239.7 all-reduce.4
